TPU v7x, 256 devices: a whole 4x4x8 slice. The times are simulated.
256 devices in a mesh: row: 128 (over y_lo, z, x, core), col: 2 (over y_hi).
Axes of the slice: x: 4, y: 4 (y_hi: 2, y_lo: 2; y = y_hi * 2 + y_lo), z: 8, core: 2. Of those that a mesh axis runs over, the one named last changes fastest.
Arguments:
- vectors: float32 [196608, 2048], P('row', 'col'), may hold values from -6 to 6
- reflectors: bfloat16 [2, 196608, 128], P('col', 'row'), may hold values from -6 to 6
- factors: bfloat16 [2, 128, 128], P('col'), may hold values from -1.804027e-05 to 0.000200336686, as said below
Outputs:
- transformed: float32 [196608, 2048], P('row', 'col')
Inputs may be any that keep to these rules, and one draw needn't show every extreme that they name: Each factors[b] is upper triangular with a positive diagonal.
All inputs are finite; a program needn't handle non-finite values.
Results may differ from a plain program's by a relative error of at most 0.0003.
Values may be sent and summed in bfloat16 or wider, within the bound.
A program may use at most 64 MiB of HBM per device.

v0:
```python
import jax
import jax.numpy as jnp
from jax import lax
from jax.sharding import PartitionSpec as P


def product(left, right):
    return jnp.dot(left, right, precision=lax.Precision.HIGHEST)


def unpack(block, rows):
    return (block[:rows].astype(jnp.float32), block[rows:].astype(jnp.float32))


def reduce_block(partial_sum, triang):
    summed = lax.psum(partial_sum, "row")
    return product(triang, summed)


def body(vectors, reflectors, factors):
    rows = reflectors.shape[1]
    packed = jnp.concatenate([reflectors, factors], axis=1)
    gathered = lax.all_gather(packed, "col", axis=0, tiled=True)
    second_block = gathered[1]
    first_block = gathered[0]
    reflect_one, triang_one = unpack(second_block, rows)
    current = vectors
    partial_one = product(reflect_one.T, current)
    applied_one = reduce_block(partial_one, triang_one)
    reflect_zero, triang_zero = unpack(first_block, rows)
    current = current - product(reflect_one, applied_one)
    partial_zero = product(reflect_zero.T, current)
    applied_zero = reduce_block(partial_zero, triang_zero)
    current = current - product(reflect_zero, applied_zero)
    return current


def solution(mesh):
    return jax.shard_map(
        body,
        mesh=mesh,
        in_specs=(P("row", "col"), P("col", "row", None), P("col", None, None)),
        out_specs=P("row", "col"),
        check_vma=False,
    )
```

profile of v0, /device:TPU:1, one launch (start us, length us, event | category | flops | bytes accessed | tf_op | source)
XLA Modules:
  0.0 2048.7 jit_solution(15938298292705342103)
XLA Ops:
  6.5 0.0 all-reduce.3.cloned.1.call-start
  6.5 1.0 pad_maximum_fusion
  7.6 12.9 all_gather.3
  20.5 5.9 fusion
  26.4 0.0 all-reduce.3.cloned.1.call-update
  26.4 0.0 all-reduce.5.cloned.1.call-start
  26.5 1000.3 %all-reduce.3.cloned.1.call-done = f32[128,1024]{1,0:T(8,128)} async-done(((f32[128,1024]{1,0:T(8,128)}), f32[128,1024]{1,0:T(8,128)}) %all-reduce.3.cloned.1.call-update) | async-done | bytes 524304 | tf_op jit(solution)/shard_map/psum | solution.py:16
  1026.8 1.4 fusion.3
  1028.2 4.9 convolution_subtract_fusion.1
  1033.2 0.0 copy-start
  1033.2 2.7 copy-done
  1035.9 3.1 fusion.1
  1039.0 0.0 all-reduce.5.cloned.1.call-update
  1039.0 995.0 %all-reduce.5.cloned.1.call-done = f32[128,1024]{1,0:T(8,128)} async-done(((f32[128,1024]{1,0:T(8,128)}), f32[128,1024]{1,0:T(8,128)}) %all-reduce.5.cloned.1.call-update) | async-done | bytes 524304 | tf_op jit(solution)/shard_map/psum | solution.py:16
  2034.0 1.4 fusion.2
  2035.4 6.4 convolution_subtract_fusion
Async XLA Ops:
  6.5 1020.3 %all-reduce.3.cloned.1.call-start = ((), (), s32[]{:S(2)}) async-start(), calls=%async_computation | async-start | bytes 1048576 | tf_op jit(solution)/shard_map/psum | solution.py:16
  26.4 2007.6 %all-reduce.5.cloned.1.call-start = ((), (), s32[]{:S(2)}) async-start(), calls=%async_computation.1 | async-start | bytes 1048576 | tf_op jit(solution)/shard_map/psum | solution.py:16
  1033.2 2.7 copy-start
Sparse Core Ops, SparseCore 0:
  26.5 1000.2 all-reduce.2
  1039.1 994.8 all-reduce.4
where the time goes:
time: 2050 us
  waiting for transfers between devices  2000 us (98%)
  matrix products  23.2 us (1%)
    psum x2, waiting for transfers between devices, reduce_block(): summed = lax.psum(partial_sum, 'row')  2000 us
  transfers between devices with their start and end apart: 2, of which 2 were waited for; matrix products, arithmetic and copies ran while one was open for 0% of the time, Pallas kernels for 0%

commit v1 on v0

v1 whole, which is shorter than its diff:
```python
import functools

import jax
import jax.numpy as jnp
from jax import lax
from jax.experimental import pallas as pl
from jax.experimental.pallas import tpu as pltpu
from jax.sharding import PartitionSpec as P

MESH = pl.DeviceIdType.MESH
F32 = jnp.float32
BF16 = jnp.bfloat16
ROWS, COLS, NB = 1536, 1024, 128
TILE = 256
VLIM = 40
BLOCK = 256
JOBS = (
    ("own", 0, 128, 0, 512, False, False),
    ("own", 0, 128, 512, 512, False, False),
    ("other", 0, 64, 0, 1024, False, False),
    ("other", 64, 48, 0, 1024, False, False),
    ("other", 112, 16, 0, 1024, True, True),
)
OTHER = (2, 3, 4)
ORDER = (
    ("c", 0), ("c", 1), (1, 0), (1, 1), ("c", 2), (2, 0), (1, 2), ("c", 3), (2, 1), ("c", 4), (1, 3), (2, 2), (3, 0), (2, 3), (2, 4),
    (3, 1), (3, 2), (4, 0), (4, 1), (3, 3), (3, 4), (5, 0), (5, 1), ("f", 0), (4, 2), (5, 2), (4, 3), (5, 4), (5, 3),
)


def tiles_of(job):
    return job[2] // 8 * (job[4] // 128) + (16 if job[5] else 0)


def split(value):
    high = value.astype(BF16)
    return high, (value - high.astype(F32)).astype(BF16)


def dot(a, b):
    return jnp.dot(a, b, preferred_element_type=F32)


def dot3(a, b):
    ah, al = split(a)
    bh, bl = split(b)
    return dot(ah, bh) + dot(ah, bl) + dot(al, bh)


def dot2(a, b):
    bh, bl = split(b)
    return dot(a, bh) + dot(a, bl)


def reduce_kernel(x_hbm, v_hbm, t_hbm, xf, yh_ref, yl_ref, v_out, *scratch):
    (v_ref, t_ref, xh, xl, vt_own, vt_oth, t_oth, a_own, in_sem, v_send, v_recv, s_send, s_recv), bufs = scratch[:13], scratch[13:]
    per = [bufs[i * 5 : i * 5 + 5] for i in range(len(JOBS))]
    row = lax.axis_index("row")
    col = lax.axis_index("col")
    core = lax.rem(row, 2)
    x = lax.rem(row // 2, 4)
    z = lax.rem(row // 8, 8)
    y = row // 64
    place = x * 2 + y
    place16 = core * 8 + place

    def at(y, z, x, core):
        return {"row": ((y * 8 + z) * 4 + x) * 2 + core, "col": col}

    partner = {"row": row, "col": 1 - col}
    sibling = at(y, z, x, 1 - core)
    v_load = pltpu.make_async_copy(v_hbm.at[0], v_ref, in_sem.at[COLS // TILE])
    v_load.start()
    t_load = pltpu.make_async_copy(t_hbm.at[0], t_ref, in_sem.at[COLS // TILE + 1])
    t_load.start()
    loads = []
    for t in range(COLS // TILE):
        part = (slice(None), pl.ds(t * TILE, TILE))
        load = pltpu.make_async_copy(x_hbm.at[part], xf.at[part], in_sem.at[t])
        load.start()
        loads.append(load)

    barrier = pltpu.get_barrier_semaphore()
    peers = [partner, sibling]
    for k in range(1, 8):
        p = lax.rem(place + k, 8)
        peers += [at(lax.rem(p, 2), z, p // 2, c) for c in (core, 1 - core)]
    peers += [at(y, lax.rem(z + k, 8), x, core) for k in range(1, 8)]
    for peer in peers:
        pl.semaphore_signal(barrier, inc=1, device_id=peer, device_id_type=MESH)
    v_load.wait()
    vt_own[...] = v_ref[...].T
    t_load.wait()
    pl.semaphore_wait(barrier, len(peers))

    def remote(src, dst, send, recv, peer):
        return pltpu.make_async_remote_copy(
            src_ref=src, dst_ref=dst, send_sem=send, recv_sem=recv, device_id=peer, device_id_type=MESH
        )

    v_copies = []
    for i, job in enumerate(OTHER):
        part = pl.ds(JOBS[job][1], JOBS[job][2])
        v_copies.append(remote(vt_own.at[part], vt_oth.at[part], v_send.at[i], v_recv.at[i], partner))
    v_copies.append(remote(t_ref, t_oth, v_send.at[len(OTHER)], v_recv.at[len(OTHER)], partner))
    for copy in v_copies:
        copy.start()

    def drain(ref, count, sem):
        part = ref.at[pl.ds(0, count)]
        pltpu.make_async_copy(part, part, sem).wait()

    def compute(j):
        block, first, count, col0, cols, gram, both = JOBS[j]
        part_ref = per[j][0]
        r8 = count // 8
        if block == "other":
            v_copies[OTHER.index(j)].wait_recv()
        for t in range(col0 // TILE, (col0 + cols) // TILE):
            cs = pl.ds(t * TILE, TILE)
            if block == "own":
                loads[t].wait()
                high, low = split(xf[:, cs])
                xh[:, cs] = high
                xl[:, cs] = low
                lhs = vt_own[pl.ds(first, count), :]
            else:
                high, low = xh[:, cs], xl[:, cs]
                lhs = vt_oth[pl.ds(first, count), :]
            value = dot(lhs, high) + dot(lhs, low)
            for s in range(TILE // 128):
                base = ((t * TILE - col0) // 128 + s) * r8
                part_ref[pl.ds(base, r8)] = value[:, s * 128 : (s + 1) * 128].reshape(r8, 8, 128)
        if gram:
            value = dot(vt_oth[...], v_ref[...])
            part_ref[pl.ds(tiles_of(JOBS[j]) - 16, 16)] = value.reshape(16, 8, 128)
        half = tiles_of(JOBS[j]) // 2
        if both:
            q = half // 8
            rx = per[j][2]
            spread(j, 1, lambda p: (part_ref.at[pl.ds(p * q, q)], rx.at[pl.ds(place16 * q, q)]))
            rx[pl.ds(place16 * q, q)] = part_ref[pl.ds(place16 * q, q)]
        else:
            remote(part_ref.at[pl.ds((1 - core) * half, half)], per[j][1], s_send.at[j, 0], s_recv.at[j, 0], sibling).start()

    def spread(j, phase, refs):
        n = group(j)
        for k in range(1, n):
            p = lax.rem(place + k, 8)
            c = core if k < 8 else 1 - core
            src, dst = refs(c * 8 + p)
            remote(src, dst, s_send.at[j, phase], s_recv.at[j, phase], at(lax.rem(p, 2), z, p // 2, c)).start()

    def group(j):
        return 16 if JOBS[j][6] else 8

    def counts(j):
        n = tiles_of(JOBS[j])
        q = n // 16
        g = group(j)
        core_hop = 0 if g == 16 else n // 2
        return (core_hop, (g - 1) * q, 7 * q, (g - 1) * q, core_hop)

    def arrived(j, phase, ref):
        drain(ref, counts(j)[phase], s_recv.at[j, phase])

    def total_of(ref, slots, q):
        total = ref[pl.ds(0, q)]
        for k in range(1, slots):
            total = total + ref[pl.ds(k * q, q)]
        return total

    def stage1(j):
        part_ref, got, rx, rz, fin = per[j]
        half = tiles_of(JOBS[j]) // 2
        q = half // 8
        arrived(j, 0, got)
        got[...] = got[...] + part_ref[pl.ds(core * half, half)]
        spread(j, 1, lambda p: (got.at[pl.ds((p - core * 8) * q, q)], rx.at[pl.ds(place * q, q)]))
        rx[pl.ds(place * q, q)] = got[pl.ds(place * q, q)]

    def stage2(j):
        part_ref, got, rx, rz, fin = per[j]
        q = tiles_of(JOBS[j]) // 16
        arrived(j, 1, rx)
        slot = pl.ds(z * q, q)
        rz[slot] = total_of(rx, group(j), q)
        for k in range(1, 8):
            zz = lax.rem(z + k, 8)
            remote(rz.at[slot], rz.at[slot], s_send.at[j, 2], s_recv.at[j, 2], at(y, zz, x, core)).start()

    def stage3(j):
        part_ref, got, rx, rz, fin = per[j]
        q = tiles_of(JOBS[j]) // 16
        arrived(j, 2, rz)
        slot = pl.ds(place16 * q, q)
        fin[slot] = total_of(rz, 8, q)
        spread(j, 3, lambda p: (fin.at[slot], fin.at[slot]))

    def stage4(j):
        fin = per[j][4]
        half = tiles_of(JOBS[j]) // 2
        arrived(j, 3, fin)
        mine = pl.ds(core * half, half)
        remote(fin.at[mine], fin.at[mine], s_send.at[j, 4], s_recv.at[j, 4], sibling).start()

    def stage5(j):
        arrived(j, 3 if JOBS[j][6] else 4, per[j][4])

    def columns(jobs_of, t):
        pieces = []
        for s in range(TILE // 128):
            parts = []
            for j, k in jobs_of(t * (TILE // 128) + s):
                count = JOBS[j][2]
                parts.append(per[j][4][pl.ds(k * (count // 8), count // 8)].reshape(count, 128))
            pieces.append(parts[0] if len(parts) == 1 else jnp.concatenate(parts, axis=0))
        return jnp.concatenate(pieces, axis=1)

    def apply_own(_):
        for t in range(COLS // TILE):
            w_own = columns(lambda k: [(k // 4, k % 4)], t)
            a_own[:, pl.ds(t * TILE, TILE)] = dot2(t_ref[...], w_own)

    run = {"c": compute, 1: stage1, 2: stage2, 3: stage3, 4: stage4, 5: stage5, "f": apply_own}
    for stage, j in ORDER:
        run[stage](j)
        if (stage, j) == (1, 3):
            v_out[:, :NB] = v_ref[...]
            v_out[:, NB:] = vt_oth[...].T
            v_copies[len(OTHER)].wait_recv()

    first = col == 0
    last = JOBS[OTHER[-1]]
    gram = per[OTHER[-1]][4][pl.ds(tiles_of(last) - 16, 16)].reshape(NB, NB)
    gram = jnp.where(first, gram.T, gram)
    t_zero = jnp.where(first, t_ref[...].astype(F32), t_oth[...].astype(F32)).astype(BF16)
    mh, ml = split(dot2(t_zero, gram))
    for t in range(COLS // TILE):
        cs = pl.ds(t * TILE, TILE)
        own = a_own[:, cs]
        oth = dot2(t_oth[...], columns(lambda k: [(j, k) for j in OTHER], t))
        y_one = jnp.where(first, oth, own)
        yh, yl = split(y_one)
        y_zero = jnp.where(first, own, oth) - (dot(mh, yh) + dot(mh, yl) + dot(ml, yh))
        y_own = jnp.where(first, y_zero, y_one)
        y_oth = jnp.where(first, y_one, y_zero)
        for base, value in ((0, y_own), (NB, y_oth)):
            high, low = split(value)
            yh_ref[pl.ds(base, NB), cs] = high
            yl_ref[pl.ds(base, NB), cs] = low

    for copy in v_copies:
        copy.wait_send()
    for j in range(len(JOBS)):
        for phase, count in enumerate(counts(j)):
            if count:
                drain(per[j][0], count, s_send.at[j, phase])


def update_kernel(x_ref, v_ref, yh_ref, yl_ref, o_hbm, out, sem):
    copies = []
    for i in range(ROWS // BLOCK):
        part = pl.ds(i * BLOCK, BLOCK)
        v = v_ref[part, :]
        out[part, :] = x_ref[part, :] - (dot(v, yh_ref[...]) + dot(v, yl_ref[...]))
        copy = pltpu.make_async_copy(out.at[part], o_hbm.at[part], sem.at[i])
        copy.start()
        copies.append(copy)
    for copy in copies:
        copy.wait()


def body(vectors, reflectors, factors):
    vmem = pl.BlockSpec(memory_space=pltpu.VMEM)
    scratch = [
        pltpu.VMEM((ROWS, NB), BF16),
        pltpu.VMEM((NB, NB), BF16),
        pltpu.VMEM((ROWS, COLS), BF16),
        pltpu.VMEM((ROWS, COLS), BF16),
        pltpu.VMEM((NB, ROWS), BF16),
        pltpu.VMEM((NB, ROWS), BF16),
        pltpu.VMEM((NB, NB), BF16),
        pltpu.VMEM((NB, COLS), F32),
        pltpu.SemaphoreType.DMA((COLS // TILE + 2,)),
        pltpu.SemaphoreType.DMA((len(OTHER) + 1,)),
        pltpu.SemaphoreType.DMA((len(OTHER) + 1,)),
        pltpu.SemaphoreType.DMA((len(JOBS), 5)),
        pltpu.SemaphoreType.DMA((len(JOBS), 5)),
    ]
    for job in JOBS:
        n = tiles_of(job)
        for count in (n, n // 2, n if job[6] else n // 2, n // 2, n):
            scratch.append(pltpu.VMEM((count, 8, 128), F32))
    hbm = pl.BlockSpec(memory_space=pltpu.HBM)
    vectors, y_high, y_low, v_all = pl.pallas_call(
        reduce_kernel,
        out_shape=(
            pltpu.VMEM((ROWS, COLS), F32),
            pltpu.VMEM((2 * NB, COLS), BF16),
            pltpu.VMEM((2 * NB, COLS), BF16),
            pltpu.VMEM((ROWS, 2 * NB), BF16),
        ),
        in_specs=[hbm, hbm, hbm],
        out_specs=(vmem, vmem, vmem, vmem),
        scratch_shapes=scratch,
        compiler_params=pltpu.CompilerParams(collective_id=0, has_side_effects=True, vmem_limit_bytes=VLIM << 20),
        cost_estimate=pl.CostEstimate(flops=2 * ROWS * COLS * 256 * 2, bytes_accessed=ROWS * COLS * 4, transcendentals=0),
        name="reduce",
    )(*(pltpu.with_memory_space_constraint(a, pltpu.HBM) for a in (vectors, reflectors, factors)))
    return pl.pallas_call(
        update_kernel,
        out_shape=jax.ShapeDtypeStruct((ROWS, COLS), F32),
        in_specs=[vmem, vmem, vmem, vmem],
        out_specs=hbm,
        scratch_shapes=[pltpu.VMEM((ROWS, COLS), F32), pltpu.SemaphoreType.DMA((ROWS // BLOCK,))],
        cost_estimate=pl.CostEstimate(flops=2 * ROWS * COLS * 512, bytes_accessed=ROWS * COLS * 8, transcendentals=0),
        compiler_params=pltpu.CompilerParams(vmem_limit_bytes=24 << 20),
        name="update",
    )(vectors, v_all, y_high, y_low)


def solution(mesh):
    return jax.shard_map(
        body,
        mesh=mesh,
        in_specs=(P("row", "col"), P("col", "row", None), P("col", None, None)),
        out_specs=P("row", "col"),
        check_vma=False,
    )
```

time: 2050 us -> 47.5 us (0.02)
  waiting for transfers between devices: 2000 us -> 0 us
  Pallas kernels: 0 us -> 47.5 us
  matrix products: 23.2 us -> 0 us
    psum x2 -> x0, waiting for transfers between devices: 2000 us -> none  [reduce_block(): summed = lax.psum(partial_sum, 'row')]
    pallas_call x0 -> x2, Pallas kernels: none -> 47.5 us  [the longest x1 44.3 us: body(): pl.pallas_call(reduce_kernel, out_shape=(pltpu.VMEM((ROWS, COLS), F32), p...]
    dot_general x6 -> x0, matrix products: 23.2 us -> none  [product(): return jnp.dot(left, right, precision=lax.Precision.HIGHEST)]
  transfers between devices with their start and end apart: 2 -> 0, of which waited for: 2 -> 0; matrix products, arithmetic and copies ran while one was open for 0% -> 0% of each run, Pallas kernels for 0% -> 0%
where the time goes in v1:
time: 47.5 us
  Pallas kernels  47.5 us (100%)
    pallas_call x1, Pallas kernels, body(): pl.pallas_call(reduce_kernel, out_shape=(pltpu.VMEM((ROWS, COLS), F32), p...  44.3 us
    pallas_call x1, Pallas kernels, body(): pl.pallas_call(update_kernel, out_shape=jax.ShapeDtypeStruct((ROWS, COLS)...  3.16 us

profile of v1, /device:TPU:1, one launch (start us, length us, event | category | flops | bytes accessed | tf_op | source)
XLA Modules:
  0.0 47.5 jit_solution(2008026314368091823)
XLA Ops:
  0.0 44.3 %reduce.1 = (f32[1536,1024]{1,0:T(8,128)S(1)}, bf16[256,1024]{1,0:T(8,128)(2,1)S(1)}, bf16[256,1024]{1,0:T(8,128)(2,1)S(1)}, bf16[1536,256]{1,0:T(8,128)(2,1)S(1)}) custom-call(f32[1536,1024]{1,0:T(8,128)} %x_hbm.1, bf16[1,1536,128]{2,1,0:T(8,128)(2,1)} %v_hbm.1, bf16[1,128,128]{2,1,0:T(8,128)(2,1)} %t_hbm.1), custom_call_target="tpu_custom_call" | custom-call | flops 1610612736 | bytes 6291456 | tf_op jit(solution)/shard_map/reduce/pallas_call | solution.py:296
  44.3 3.2 %update.1 = f32[1536,1024]{1,0:T(8,128)} custom-call(f32[1536,1024]{1,0:T(8,128)S(1)} %get-tuple-element.9.x_ref, bf16[1536,256]{1,0:T(8,128)(2,1)S(1)} %get-tuple-element.10.v_ref, bf16[256,1024]{1,0:T(8,128)(2,1)S(1)} %get-tuple-element.11.yh_ref, bf16[256,1024]{1,0:T(8,128)(2,1)S(1)} %get-tuple-element.12.yl_ref), custom_call_target="tpu_custom_call" | custom-call | flops 1610612736 | bytes 12582912 | tf_op jit(solution)/shard_map/update/pallas_call | solution.py:311

commit v2 on v1

--- a/solution.py
+++ b/solution.py
@@ -13,7 +13,7 @@
 ROWS, COLS, NB = 1536, 1024, 128
 TILE = 256
 VLIM = 40
-BLOCK = 256
+BLOCKS = ((0, 768), (768, 512), (1280, 256))
 JOBS = (
     ("own", 0, 128, 0, 512, False, False),
     ("own", 0, 128, 512, 512, False, False),
@@ -21,11 +21,21 @@
     ("other", 64, 48, 0, 1024, False, False),
     ("other", 112, 16, 0, 1024, True, True),
 )
+OWN = (0, 1)
 OTHER = (2, 3, 4)
 ORDER = (
     ("c", 0), ("c", 1), (1, 0), (1, 1), ("c", 2), (2, 0), (1, 2), ("c", 3), (2, 1), ("c", 4), (1, 3), (2, 2), (3, 0), (2, 3), (2, 4),
     (3, 1), (3, 2), (4, 0), (4, 1), (3, 3), (3, 4), (5, 0), (5, 1), ("f", 0), (4, 2), (5, 2), (4, 3), (5, 4), (5, 3),
 )
+
+
+PLANE = tuple(
+    (dx, dy, dc)
+    for dx, dy in ((2, 1), (1, 1), (3, 1), (2, 0), (1, 0), (3, 0), (0, 1), (0, 0))
+    for dc in (1, 0)
+    if dx or dy or dc
+)
+LINE = (4, 3, 5, 2, 6, 1, 7)
 
 
 def tiles_of(job):
@@ -71,6 +81,12 @@
     sibling = at(y, z, x, 1 - core)
     v_load = pltpu.make_async_copy(v_hbm.at[0], v_ref, in_sem.at[COLS // TILE])
     v_load.start()
+    barrier = pltpu.get_barrier_semaphore()
+    peers = [at(lax.rem(y + dy, 2), z, lax.rem(x + dx, 4), lax.rem(core + dc, 2)) for dx, dy, dc in PLANE]
+    peers.insert(4, partner)
+    peers += [at(y, lax.rem(z + k, 8), x, core) for k in LINE]
+    for peer in peers:
+        pl.semaphore_signal(barrier, inc=1, device_id=peer, device_id_type=MESH)
     t_load = pltpu.make_async_copy(t_hbm.at[0], t_ref, in_sem.at[COLS // TILE + 1])
     t_load.start()
     loads = []
@@ -79,15 +95,6 @@
         load = pltpu.make_async_copy(x_hbm.at[part], xf.at[part], in_sem.at[t])
         load.start()
         loads.append(load)
-
-    barrier = pltpu.get_barrier_semaphore()
-    peers = [partner, sibling]
-    for k in range(1, 8):
-        p = lax.rem(place + k, 8)
-        peers += [at(lax.rem(p, 2), z, p // 2, c) for c in (core, 1 - core)]
-    peers += [at(y, lax.rem(z + k, 8), x, core) for k in range(1, 8)]
-    for peer in peers:
-        pl.semaphore_signal(barrier, inc=1, device_id=peer, device_id_type=MESH)
     v_load.wait()
     vt_own[...] = v_ref[...].T
     t_load.wait()
@@ -144,12 +151,13 @@
             remote(part_ref.at[pl.ds((1 - core) * half, half)], per[j][1], s_send.at[j, 0], s_recv.at[j, 0], sibling).start()
 
     def spread(j, phase, refs):
-        n = group(j)
-        for k in range(1, n):
-            p = lax.rem(place + k, 8)
-            c = core if k < 8 else 1 - core
-            src, dst = refs(c * 8 + p)
-            remote(src, dst, s_send.at[j, phase], s_recv.at[j, phase], at(lax.rem(p, 2), z, p // 2, c)).start()
+        for dx, dy, dc in PLANE:
+            if dc and group(j) == 8:
+                continue
+            to = at(lax.rem(y + dy, 2), z, lax.rem(x + dx, 4), lax.rem(core + dc, 2))
+            p = lax.rem(core + dc, 2) * 8 + lax.rem(x + dx, 4) * 2 + lax.rem(y + dy, 2)
+            src, dst = refs(p)
+            remote(src, dst, s_send.at[j, phase], s_recv.at[j, phase], to).start()
 
     def group(j):
         return 16 if JOBS[j][6] else 8
@@ -185,7 +193,7 @@
         arrived(j, 1, rx)
         slot = pl.ds(z * q, q)
         rz[slot] = total_of(rx, group(j), q)
-        for k in range(1, 8):
+        for k in LINE:
             zz = lax.rem(z + k, 8)
             remote(rz.at[slot], rz.at[slot], s_send.at[j, 2], s_recv.at[j, 2], at(y, zz, x, core)).start()
 
@@ -219,13 +227,13 @@
 
     def apply_own(_):
         for t in range(COLS // TILE):
-            w_own = columns(lambda k: [(k // 4, k % 4)], t)
+            w_own = columns(lambda k: [(j, k - JOBS[j][3] // 128) for j in OWN if 0 <= k * 128 - JOBS[j][3] < JOBS[j][4]], t)
             a_own[:, pl.ds(t * TILE, TILE)] = dot2(t_ref[...], w_own)
 
     run = {"c": compute, 1: stage1, 2: stage2, 3: stage3, 4: stage4, 5: stage5, "f": apply_own}
     for stage, j in ORDER:
         run[stage](j)
-        if (stage, j) == (1, 3):
+        if (stage, j) == ("c", OTHER[-1]):
             v_out[:, :NB] = v_ref[...]
             v_out[:, NB:] = vt_oth[...].T
             v_copies[len(OTHER)].wait_recv()
@@ -260,8 +268,8 @@
 
 def update_kernel(x_ref, v_ref, yh_ref, yl_ref, o_hbm, out, sem):
     copies = []
-    for i in range(ROWS // BLOCK):
-        part = pl.ds(i * BLOCK, BLOCK)
+    for i, (first, count) in enumerate(BLOCKS):
+        part = pl.ds(first, count)
         v = v_ref[part, :]
         out[part, :] = x_ref[part, :] - (dot(v, yh_ref[...]) + dot(v, yl_ref[...]))
         copy = pltpu.make_async_copy(out.at[part], o_hbm.at[part], sem.at[i])
@@ -313,7 +321,7 @@
         out_shape=jax.ShapeDtypeStruct((ROWS, COLS), F32),
         in_specs=[vmem, vmem, vmem, vmem],
         out_specs=hbm,
-        scratch_shapes=[pltpu.VMEM((ROWS, COLS), F32), pltpu.SemaphoreType.DMA((ROWS // BLOCK,))],
+        scratch_shapes=[pltpu.VMEM((ROWS, COLS), F32), pltpu.SemaphoreType.DMA((len(BLOCKS),))],
         cost_estimate=pl.CostEstimate(flops=2 * ROWS * COLS * 512, bytes_accessed=ROWS * COLS * 8, transcendentals=0),
         compiler_params=pltpu.CompilerParams(vmem_limit_bytes=24 << 20),
         name="update",

time: 47.5 us -> 46.5 us (0.979)
  Pallas kernels: 47.5 us -> 46.4 us
    pallas_call x1, Pallas kernels: 44.3 us -> 42.7 us  [body(): pl.pallas_call(reduce_kernel, out_shape=(pltpu.VMEM((ROWS, COLS), F32), p...]
    pallas_call x1, Pallas kernels: 3.16 us -> 3.71 us  [body(): pl.pallas_call(update_kernel, out_shape=jax.ShapeDtypeStruct((ROWS, COLS)...]
where the time goes in v2:
time: 46.5 us; the launch traced here: 46.4 us
  Pallas kernels  46.4 us (100%)
    pallas_call x1, Pallas kernels, body(): pl.pallas_call(reduce_kernel, out_shape=(pltpu.VMEM((ROWS, COLS), F32), p...  42.7 us
    pallas_call x1, Pallas kernels, body(): pl.pallas_call(update_kernel, out_shape=jax.ShapeDtypeStruct((ROWS, COLS)...  3.71 us

profile of v2, /device:TPU:1, one launch (start us, length us, event | category | flops | bytes accessed | tf_op | source)
XLA Modules:
  0.0 46.4 jit_solution(12747283692431520756)
XLA Ops:
  0.0 42.7 %reduce.1 = (f32[1536,1024]{1,0:T(8,128)S(1)}, bf16[256,1024]{1,0:T(8,128)(2,1)S(1)}, bf16[256,1024]{1,0:T(8,128)(2,1)S(1)}, bf16[1536,256]{1,0:T(8,128)(2,1)S(1)}) custom-call(f32[1536,1024]{1,0:T(8,128)} %x_hbm.1, bf16[1,1536,128]{2,1,0:T(8,128)(2,1)} %v_hbm.1, bf16[1,128,128]{2,1,0:T(8,128)(2,1)} %t_hbm.1), custom_call_target="tpu_custom_call" | custom-call | flops 1610612736 | bytes 6291456 | tf_op jit(solution)/shard_map/reduce/pallas_call | solution.py:304
  42.7 3.7 %update.1 = f32[1536,1024]{1,0:T(8,128)} custom-call(f32[1536,1024]{1,0:T(8,128)S(1)} %get-tuple-element.9.x_ref, bf16[1536,256]{1,0:T(8,128)(2,1)S(1)} %get-tuple-element.10.v_ref, bf16[256,1024]{1,0:T(8,128)(2,1)S(1)} %get-tuple-element.11.yh_ref, bf16[256,1024]{1,0:T(8,128)(2,1)S(1)} %get-tuple-element.12.yl_ref), custom_call_target="tpu_custom_call" | custom-call | flops 1610612736 | bytes 12582912 | tf_op jit(solution)/shard_map/update/pallas_call | solution.py:319

commit v3 on v2

--- a/solution.py
+++ b/solution.py
@@ -13,7 +13,7 @@
 ROWS, COLS, NB = 1536, 1024, 128
 TILE = 256
 VLIM = 40
-BLOCKS = ((0, 768), (768, 512), (1280, 256))
+BLOCKS = tuple((first, 256) for first in range(0, 1536, 256))
 JOBS = (
     ("own", 0, 128, 0, 512, False, False),
     ("own", 0, 128, 512, 512, False, False),
@@ -25,10 +25,8 @@
 OTHER = (2, 3, 4)
 ORDER = (
     ("c", 0), ("c", 1), (1, 0), (1, 1), ("c", 2), (2, 0), (1, 2), ("c", 3), (2, 1), ("c", 4), (1, 3), (2, 2), (3, 0), (2, 3), (2, 4),
-    (3, 1), (3, 2), (4, 0), (4, 1), (3, 3), (3, 4), (5, 0), (5, 1), ("f", 0), (4, 2), (5, 2), (4, 3), (5, 4), (5, 3),
+    ("v", 0), (3, 1), (3, 2), (4, 0), (4, 1), (3, 3), (3, 4), (5, 0), (5, 1), ("f", 0), (4, 2), (5, 2), (4, 3), (5, 4), ("g", 0), (5, 3),
 )
-
-
 PLANE = tuple(
     (dx, dy, dc)
     for dx, dy in ((2, 1), (1, 1), (3, 1), (2, 0), (1, 0), (3, 0), (0, 1), (0, 0))
@@ -63,7 +61,7 @@
 
 
 def reduce_kernel(x_hbm, v_hbm, t_hbm, xf, yh_ref, yl_ref, v_out, *scratch):
-    (v_ref, t_ref, xh, xl, vt_own, vt_oth, t_oth, a_own, in_sem, v_send, v_recv, s_send, s_recv), bufs = scratch[:13], scratch[13:]
+    (v_ref, t_ref, xh, xl, vt_own, vt_oth, t_oth, a_own, m_ref, in_sem, v_send, v_recv, s_send, s_recv), bufs = scratch[:14], scratch[14:]
     per = [bufs[i * 5 : i * 5 + 5] for i in range(len(JOBS))]
     row = lax.axis_index("row")
     col = lax.axis_index("col")
@@ -230,20 +228,24 @@
             w_own = columns(lambda k: [(j, k - JOBS[j][3] // 128) for j in OWN if 0 <= k * 128 - JOBS[j][3] < JOBS[j][4]], t)
             a_own[:, pl.ds(t * TILE, TILE)] = dot2(t_ref[...], w_own)
 
-    run = {"c": compute, 1: stage1, 2: stage2, 3: stage3, 4: stage4, 5: stage5, "f": apply_own}
+    first = col == 0
+
+    def hand_over(_):
+        v_out[:, :NB] = v_ref[...]
+        v_out[:, NB:] = vt_oth[...].T
+        v_copies[len(OTHER)].wait_recv()
+
+    def apply_gram(_):
+        last = OTHER[-1]
+        gram = per[last][4][pl.ds(tiles_of(JOBS[last]) - 16, 16)].reshape(NB, NB)
+        gram = jnp.where(first, gram.T, gram)
+        t_zero = jnp.where(first, t_ref[...].astype(F32), t_oth[...].astype(F32)).astype(BF16)
+        m_ref[...] = dot2(t_zero, gram)
+
+    run = {"v": hand_over, "g": apply_gram, "c": compute, 1: stage1, 2: stage2, 3: stage3, 4: stage4, 5: stage5, "f": apply_own}
     for stage, j in ORDER:
         run[stage](j)
-        if (stage, j) == ("c", OTHER[-1]):
-            v_out[:, :NB] = v_ref[...]
-            v_out[:, NB:] = vt_oth[...].T
-            v_copies[len(OTHER)].wait_recv()
-
-    first = col == 0
-    last = JOBS[OTHER[-1]]
-    gram = per[OTHER[-1]][4][pl.ds(tiles_of(last) - 16, 16)].reshape(NB, NB)
-    gram = jnp.where(first, gram.T, gram)
-    t_zero = jnp.where(first, t_ref[...].astype(F32), t_oth[...].astype(F32)).astype(BF16)
-    mh, ml = split(dot2(t_zero, gram))
+    mh, ml = split(m_ref[...])
     for t in range(COLS // TILE):
         cs = pl.ds(t * TILE, TILE)
         own = a_own[:, cs]
@@ -290,6 +292,7 @@
         pltpu.VMEM((NB, ROWS), BF16),
         pltpu.VMEM((NB, NB), BF16),
         pltpu.VMEM((NB, COLS), F32),
+        pltpu.VMEM((NB, NB), F32),
         pltpu.SemaphoreType.DMA((COLS // TILE + 2,)),
         pltpu.SemaphoreType.DMA((len(OTHER) + 1,)),
         pltpu.SemaphoreType.DMA((len(OTHER) + 1,)),

time: 46.5 us -> 45.9 us (0.987)
  Pallas kernels: 46.4 us -> 45.8 us
    pallas_call x1, Pallas kernels: 3.71 us -> 3.16 us  [body(): pl.pallas_call(update_kernel, out_shape=jax.ShapeDtypeStruct((ROWS, COLS)...]
where the time goes in v3:
time: 45.9 us; the launch traced here: 45.8 us
  Pallas kernels  45.8 us (100%)
    pallas_call x1, Pallas kernels, body(): pl.pallas_call(reduce_kernel, out_shape=(pltpu.VMEM((ROWS, COLS), F32), p...  42.6 us
    pallas_call x1, Pallas kernels, body(): pl.pallas_call(update_kernel, out_shape=jax.ShapeDtypeStruct((ROWS, COLS)...  3.16 us

profile of v3, /device:TPU:1, one launch (start us, length us, event | category | flops | bytes accessed | tf_op | source)
XLA Modules:
  0.0 45.8 jit_solution(15802191664074605090)
XLA Ops:
  0.0 42.6 %reduce.1 = (f32[1536,1024]{1,0:T(8,128)S(1)}, bf16[256,1024]{1,0:T(8,128)(2,1)S(1)}, bf16[256,1024]{1,0:T(8,128)(2,1)S(1)}, bf16[1536,256]{1,0:T(8,128)(2,1)S(1)}) custom-call(f32[1536,1024]{1,0:T(8,128)} %x_hbm.1, bf16[1,1536,128]{2,1,0:T(8,128)(2,1)} %v_hbm.1, bf16[1,128,128]{2,1,0:T(8,128)(2,1)} %t_hbm.1), custom_call_target="tpu_custom_call" | custom-call | flops 1610612736 | bytes 6291456 | tf_op jit(solution)/shard_map/reduce/pallas_call | solution.py:307
  42.6 3.2 %update.1 = f32[1536,1024]{1,0:T(8,128)} custom-call(f32[1536,1024]{1,0:T(8,128)S(1)} %get-tuple-element.9.x_ref, bf16[1536,256]{1,0:T(8,128)(2,1)S(1)} %get-tuple-element.10.v_ref, bf16[256,1024]{1,0:T(8,128)(2,1)S(1)} %get-tuple-element.11.yh_ref, bf16[256,1024]{1,0:T(8,128)(2,1)S(1)} %get-tuple-element.12.yl_ref), custom_call_target="tpu_custom_call" | custom-call | flops 1610612736 | bytes 12582912 | tf_op jit(solution)/shard_map/update/pallas_call | solution.py:322

commit v4 on v3

--- a/solution.py
+++ b/solution.py
@@ -25,7 +25,7 @@
 OTHER = (2, 3, 4)
 ORDER = (
     ("c", 0), ("c", 1), (1, 0), (1, 1), ("c", 2), (2, 0), (1, 2), ("c", 3), (2, 1), ("c", 4), (1, 3), (2, 2), (3, 0), (2, 3), (2, 4),
-    ("v", 0), (3, 1), (3, 2), (4, 0), (4, 1), (3, 3), (3, 4), (5, 0), (5, 1), ("f", 0), (4, 2), (5, 2), (4, 3), (5, 4), ("g", 0), (5, 3),
+    ("v", 0), (3, 1), (3, 2), (4, 0), (4, 1), (3, 3), (3, 4), (5, 0), (5, 1), (4, 2), (4, 3), ("f", 0), (5, 2), (5, 4), ("g", 0), (5, 3),
 )
 PLANE = tuple(
     (dx, dy, dc)
@@ -270,10 +270,11 @@
 
 def update_kernel(x_ref, v_ref, yh_ref, yl_ref, o_hbm, out, sem):
     copies = []
+    both = jnp.concatenate([yh_ref[...], yl_ref[...]], axis=0)
     for i, (first, count) in enumerate(BLOCKS):
         part = pl.ds(first, count)
         v = v_ref[part, :]
-        out[part, :] = x_ref[part, :] - (dot(v, yh_ref[...]) + dot(v, yl_ref[...]))
+        out[part, :] = x_ref[part, :] - dot(jnp.concatenate([v, v], axis=1), both)
         copy = pltpu.make_async_copy(out.at[part], o_hbm.at[part], sem.at[i])
         copy.start()
         copies.append(copy)

time: 45.9 us -> 45.9 us (level)
  no operation moved by 1% of the time
where the time goes in v4:
time: 45.9 us; the launch traced here: 45.8 us
  Pallas kernels  45.8 us (100%)
    pallas_call x1, Pallas kernels, body(): pl.pallas_call(reduce_kernel, out_shape=(pltpu.VMEM((ROWS, COLS), F32), p...  42.6 us
    pallas_call x1, Pallas kernels, body(): pl.pallas_call(update_kernel, out_shape=jax.ShapeDtypeStruct((ROWS, COLS)...  3.16 us

profile of v4, /device:TPU:1, one launch (start us, length us, event | category | flops | bytes accessed | tf_op | source)
XLA Modules:
  0.0 45.8 jit_solution(5922478853082475023)
XLA Ops:
  0.0 42.6 %reduce.1 = (f32[1536,1024]{1,0:T(8,128)S(1)}, bf16[256,1024]{1,0:T(8,128)(2,1)S(1)}, bf16[256,1024]{1,0:T(8,128)(2,1)S(1)}, bf16[1536,256]{1,0:T(8,128)(2,1)S(1)}) custom-call(f32[1536,1024]{1,0:T(8,128)} %x_hbm.1, bf16[1,1536,128]{2,1,0:T(8,128)(2,1)} %v_hbm.1, bf16[1,128,128]{2,1,0:T(8,128)(2,1)} %t_hbm.1), custom_call_target="tpu_custom_call" | custom-call | flops 1610612736 | bytes 6291456 | tf_op jit(solution)/shard_map/reduce/pallas_call | solution.py:308
  42.6 3.2 %update.1 = f32[1536,1024]{1,0:T(8,128)} custom-call(f32[1536,1024]{1,0:T(8,128)S(1)} %get-tuple-element.9.x_ref, bf16[1536,256]{1,0:T(8,128)(2,1)S(1)} %get-tuple-element.10.v_ref, bf16[256,1024]{1,0:T(8,128)(2,1)S(1)} %get-tuple-element.11.yh_ref, bf16[256,1024]{1,0:T(8,128)(2,1)S(1)} %get-tuple-element.12.yl_ref), custom_call_target="tpu_custom_call" | custom-call | flops 1610612736 | bytes 12582912 | tf_op jit(solution)/shard_map/update/pallas_call | solution.py:323
